TPU v7x, 512 devices: a whole 4x8x8 slice. The times are simulated.
512 devices in a mesh: row: 32 (over z_hi, x, core), col: 16 (over y, z_lo).
Axes of the slice: x: 4, y: 8, z: 8 (z_hi: 4, z_lo: 2; z = z_hi * 2 + z_lo), core: 2. Of those that a mesh axis runs over, the one named last changes fastest.
Arguments:
- tokens: bfloat16 [65536, 1024], P('row', 'col'), may hold values from -6 to 6
- up_weight: bfloat16 [1024, 4096], P('row', 'col'), may hold values from -0.1875 to 0.1875
- hidden_grad: bfloat16 [65536, 4096], P('row', 'col'), may hold values from -6 to 6
Outputs:
- hidden: bfloat16 [65536, 4096], P('row', 'col')
- input_grad: bfloat16 [65536, 1024], P('row', 'col')
All inputs are finite; a program needn't handle non-finite values.
Results may differ from a plain program's by a relative error of at most 0.017.
Values may be sent and summed in bfloat16 or wider, within the bound.
A program may use at most 64 MiB of HBM per device.

v0:
```python
import jax
import jax.numpy as jnp
from jax import lax
from jax.sharding import PartitionSpec as P

gelu_c = 0.7978845608028654
gelu_a = 0.044715


def gelu_value(v):
    inner = gelu_c * (v + gelu_a * v * v * v)
    return 0.5 * v * (1.0 + jnp.tanh(inner))


def gelu_slope(v):
    inner = gelu_c * (v + gelu_a * v * v * v)
    tval = jnp.tanh(inner)
    return 0.5 * (1.0 + tval) + 0.5 * v * (1.0 - tval * tval) * gelu_c * (
        1.0 + 3.0 * gelu_a * v * v
    )


def per_device(tokens, up_weight, hidden_grad):
    column_panel = lax.all_gather(up_weight, "row", axis=0, tiled=True)
    token_rows = lax.all_gather(tokens, "col", axis=1, tiled=True)
    preact = jnp.dot(token_rows, column_panel, preferred_element_type=jnp.float32)
    hidden = gelu_value(preact).astype(jnp.bfloat16)
    pre_grad = (hidden_grad.astype(jnp.float32) * gelu_slope(preact)).astype(jnp.bfloat16)
    summed = lax.psum_scatter(
        lax.dot_general(
            column_panel, pre_grad, (((1,), (1,)), ((), ())), preferred_element_type=jnp.float32
        ).astype(jnp.bfloat16),
        "col",
        scatter_dimension=0,
        tiled=True,
    ).astype(jnp.float32)
    input_grad = jnp.transpose(summed).astype(jnp.bfloat16)
    return (hidden, input_grad)


def solution(mesh):
    in_specs = (P("row", "col"), P("row", "col"), P("row", "col"))
    out_specs = (P("row", "col"), P("row", "col"))
    return jax.shard_map(
        per_device, mesh=mesh, in_specs=in_specs, out_specs=out_specs, check_vma=False
    )
```

profile of v0, /device:TPU:2, one launch (start us, length us, event | category | flops | bytes accessed | tf_op | source)
XLA Modules:
  0.0 244.5 jit_solution(7380945636394630363)
XLA Ops:
  7.2 0.0 all-gather.2.cloned.1.call-start
  7.2 0.7 all-gather.2.cloned.1.call-update
  7.9 0.0 reduce-scatter.4.cloned.1.call-start
  7.9 49.0 %all_gather.7 = bf16[1024,256]{1,0:T(8,128)(2,1)S(1)} all-gather(bf16[32,256]{1,0:T(8,128)(2,1)} %param.4), channel_id=1, replica_groups=mesh['row'=32,'col'=16] {'row'}, dimensions={0}, use_global_device_ids=true | all-gather | bytes 540672 | tf_op jit(solution)/shard_map/all_gather | solution.py:24
  57.0 0.0 copy-start
  57.0 60.6 %all-gather.2.cloned.1.call-done = bf16[2048,1024]{0,1:T(8,128)(2,1)} async-done(((bf16[2048,64]{0,1:T(8,128)(2,1)}), bf16[2048,1024]{0,1:T(8,128)(2,1)}) %all-gather.2.cloned.1.call-update) | async-done | bytes 4194320 | tf_op jit(solution)/shard_map/all_gather | solution.py:25
  117.6 4.8 %multiply_convert_fusion = (bf16[2048,256]{1,0:T(8,128)(2,1)}, f32[2048,256]{1,0:T(8,128)S(1)}) fusion(bf16[2048,1024]{0,1:T(8,128)(2,1)} %all-gather.2.cloned.1.call-done, bf16[1024,256]{1,0:T(8,128)(2,1)S(1)} %all_gather.7), kind=kOutput, calls=%fused_computation.10 | convolution fusion | flops 1078460416 | bytes 7864320 | tf_op jit(solution)/shard_map/dot_general | solution.py:26
  122.3 0.0 copy-done
  122.4 3.7 %convert_bitcast_fusion = bf16[1024,2048]{0,1:T(8,128)(2,1)} fusion(bf16[1024,256]{1,0:T(8,128)(2,1)S(1)} %all_gather.7, f32[2048,256]{1,0:T(8,128)S(1)} %get-tuple-element.7, bf16[2048,256]{1,0:T(8,128)(2,1)S(1)} %copy-done), kind=kOutput, calls=%fused_computation | convolution fusion | flops 1086324736 | bytes 7864320 | tf_op jit(solution)/shard_map/dot_general | solution.py:30
  126.0 6.5 %copy.7 = bf16[1024,2048]{1,0:T(8,128)(2,1)} copy(bf16[1024,2048]{0,1:T(8,128)(2,1)} %convert_bitcast_fusion) | data formatting | bytes 8388608
  132.6 0.0 reduce-scatter.4.cloned.1.call-update
  132.6 105.1 %reduce-scatter.4.cloned.1.call-done = bf16[64,2048]{1,0:T(8,128)(2,1)} async-done(((bf16[1024,2048]{1,0:T(8,128)(2,1)}), bf16[64,2048]{1,0:T(8,128)(2,1)}) %reduce-scatter.4.cloned.1.call-update) | async-done | bytes 262160
Async XLA Ops:
  7.2 110.4 %all-gather.2.cloned.1.call-start = ((), (), s32[]{:S(2)}) async-start(), calls=%async_computation.1 | async-start | bytes 4456448 | tf_op jit(solution)/shard_map/all_gather | solution.py:25
  7.9 229.7 %reduce-scatter.4.cloned.1.call-start = ((), (), s32[]{:S(2)}) async-start(), calls=%async_computation.2 | async-start | bytes 4456448
  57.0 65.4 %copy-start = (bf16[2048,256]{1,0:T(8,128)(2,1)S(1)}, bf16[2048,256]{1,0:T(8,128)(2,1)}, u32[]{:S(2)}) copy-start(bf16[2048,256]{1,0:T(8,128)(2,1)} %param.5) | copy-start | bytes 3145732
Sparse Core Ops, SparseCore 0:
  10.1 107.4 all-gather.1
  132.7 104.8 reduce-scatter.3
where the time goes:
time: 245 us; the launch traced here: 244 us
  waiting for transfers between devices  166 us (68%)
  blocking collectives  49 us (20%)
  between operations  14 us (6%)
  matrix products  8.46 us (3%)
  local copies, waits for them, and re-layouts  6.53 us (3%)
    unnamed x3, waiting for transfers between devices  106 us
    all_gather x1, waiting for transfers between devices, per_device(): token_rows = lax.all_gather(tokens, 'col', axis=1, tiled=True)  60.6 us
    all_gather x1, blocking collectives, per_device(): column_panel = lax.all_gather(up_weight, 'row', axis=0, tiled=True)  49 us
    unnamed x3, local copies, waits for them, and re-layouts  6.53 us
  transfers between devices with their start and end apart: 2, of which 2 were waited for; matrix products, arithmetic and copies ran while one was open for 0% of the time, Pallas kernels for 0%

commit v1 on v0

v1 whole, which is shorter than its diff:
```python
import jax
import jax.numpy as jnp
from jax import lax
from jax.experimental import pallas as pl
from jax.experimental.pallas import tpu as pltpu
from jax.sharding import PartitionSpec as P

gelu_c = 0.7978845608028654
gelu_a = 0.044715

NZH, NX, NY = 4, 4, 8
NZ = 2 * NZH
CHUNKS = 4
MESH = pl.DeviceIdType.MESH
UP, DOWN = 0, 1


def chain(way, k):
    return NY // 2 if (k % 2 == 0) == (way == UP) else NY // 2 - 1


def kernel(
    tok_in, w_in, grad_in, hid_out, ig_out,
    tok_t, tok, wb, grad, hid, pre, pg, part, rs, fin,
    load_sem, tx_send, tx_recv, wz_send, wz_recv, wx_send, wx_recv, wc_send, wc_recv,
    hg_send, hg_recv, ag_send, ag_recv, rs_send, rs_recv, ho_send, ho_recv, io_send, io_recv, store_sem,
):
    feats, half = tok_in.shape[0], tok_in.shape[1] // 2
    size = half // CHUNKS
    wide = 2 * feats
    r, c = lax.axis_index("row"), lax.axis_index("col")
    y, zl = lax.div(c, 2), lax.rem(c, 2)
    zh, x, core = lax.div(r, 2 * NX), lax.rem(lax.div(r, 2), NX), lax.rem(r, 2)
    zo = 1 - zl
    z = 2 * zh + zl
    mine = pl.multiple_of(zl * half, half)
    other = pl.multiple_of(zo * half, half)

    def at_y(step):
        return lax.rem(y + step + NY, NY)

    def z_device(step):
        there = lax.rem(z + step, NZ)
        return ((lax.div(there, 2) * NX + x) * 2 + core, 2 * y + lax.rem(there, 2))

    def x_device(step):
        return ((zh * NX + lax.rem(x + step, NX)) * 2 + core, c)

    ring = ((r, 2 * at_y(1) + zl), (r, 2 * at_y(-1) + zl))
    partner = (r, c + 1 - 2 * zl)
    sibling = (r + 1 - 2 * core, c)

    def remote(src, dst, send, recv, device):
        return pltpu.make_async_remote_copy(
            src_ref=src, dst_ref=dst, send_sem=send, recv_sem=recv, device_id=device, device_id_type=MESH
        )

    loads = [
        pltpu.make_async_copy(
            tok_in.at[:, pl.ds(mine, half)], tok_t.at[pl.ds(pl.multiple_of(zl * feats, feats), feats)], load_sem.at[0]
        ),
        pltpu.make_async_copy(w_in, wb.at[zl, zh, x, core], load_sem.at[1]),
        pltpu.make_async_copy(grad_in.at[pl.ds(mine, half)], grad.at[zl], load_sem.at[2]),
    ]
    for load in loads:
        load.start()

    barrier = pltpu.get_barrier_semaphore()
    peers = [z_device(d) for d in range(1, NZ)] + [x_device(d) for d in range(1, NX)] + [*ring, sibling]
    for peer in peers:
        pl.semaphore_signal(barrier, inc=1, device_id=peer, device_id_type=MESH)
    pl.semaphore_wait(barrier, len(peers))

    sent = []

    def start(copy):
        copy.start()
        sent.append(copy)
        return copy

    tx = []
    for k in range(CHUNKS):
        there = pl.ds(pl.multiple_of(other + k * size, size), size)
        tx.append(
            start(
                remote(
                    tok_in.at[:, there],
                    tok_t.at[pl.ds(pl.multiple_of(zl * feats, feats), feats), pl.ds(k * size, size)],
                    tx_send.at[k], tx_recv.at[k], partner,
                )
            )
        )
    wz = [
        start(remote(w_in, wb.at[zl, zh, x, core], wz_send.at[d - 1], wz_recv.at[d - 1], z_device(d)))
        for d in range(1, NZ)
    ]

    def ag_copy(way, k, s):
        shard = tok.at[at_y(1 - s if way == UP else s - 1), pl.ds(k * size, size)]
        return remote(shard, shard, ag_send.at[way, k, s - 1], ag_recv.at[way, k, s - 1], ring[way])

    ag = {}
    loads[0].wait()
    for k in range(CHUNKS):
        tx[k].wait_recv()
        tok[y, k * size : (k + 1) * size, :] = jnp.transpose(tok_t[:, k * size : (k + 1) * size])
        for way in (UP, DOWN):
            ag[way, k, 1] = start(ag_copy(way, k, 1))

    def ag_step(k, s):
        for way in (UP, DOWN):
            if s <= chain(way, k):
                ag[way, k, s].wait_recv()
            if s < chain(way, k):
                ag[way, k, s + 1] = start(ag_copy(way, k, s + 1))

    hg = []
    for k in range(CHUNKS):
        here = pl.ds(pl.multiple_of(other + k * size, size), size)
        hg.append(
            start(remote(grad_in.at[here], grad.at[zl, pl.ds(k * size, size)], hg_send.at[k], hg_recv.at[k], partner))
        )

    loads[1].wait()
    for copy in wz:
        copy.wait_recv()
    wx = [
        start(remote(wb.at[:, :, x, core], wb.at[:, :, x, core], wx_send.at[d - 1], wx_recv.at[d - 1], x_device(d)))
        for d in range(1, NX)
    ]

    def to_sibling(d):
        block = wb.at[:, :, lax.rem(x + NX - d, NX), core]
        return start(remote(block, block, wc_send.at[d], wc_recv.at[d], sibling))

    wc = [to_sibling(0)]
    for k in range(CHUNKS):
        ag_step(k, 1)
    for d in range(1, NX):
        wx[d - 1].wait_recv()
        wc.append(to_sibling(d))
    for s in range(2, NY // 2):
        for k in range(CHUNKS):
            ag_step(k, s)
    for copy in wc:
        copy.wait_recv()
    loads[2].wait()

    depth, units = NY * wide, w_in.shape[1]

    def compute(k):
        rows = pl.ds(k * size, size)
        left = jnp.concatenate([tok[j, rows, :] for j in range(NY)], axis=1)
        for b in range(2):
            pre[b] = jnp.dot(left, wb[b].reshape(depth, units), preferred_element_type=jnp.float32)

        @pl.loop(0, size // 16)
        def _(i):
            for b in range(2):
                v = pre[b, pl.ds(pl.multiple_of(i * 16, 16), 16), :]
                u = v * v
                t = jnp.tanh(v * (gelu_c + gelu_c * gelu_a * u))
                h = 0.5 + 0.5 * t
                slope = h + (0.5 * v) * (1.0 - t * t) * (gelu_c + 3.0 * gelu_c * gelu_a * u)
                at = pl.ds(pl.multiple_of(k * size + i * 16, 16), 16)
                hid[b, at, :] = (v * h).astype(jnp.bfloat16)
                pg[pl.ds(pl.multiple_of(i * 16, 16), 16), b * units : (b + 1) * units] = (
                    grad[b, at, :].astype(jnp.float32) * slope
                ).astype(jnp.bfloat16)

        weights = jnp.concatenate([wb[b].reshape(depth, units) for b in range(2)], axis=1)
        part[k] = lax.dot_general(
            weights, pg[...], (((1,), (1,)), ((), ())), preferred_element_type=jnp.float32
        ).astype(jnp.bfloat16)

    def rs_rows(way, k, s):
        far = chain(way, k) - s + 1
        return pl.ds(pl.multiple_of(at_y(far if way == UP else -far) * wide, wide), wide)

    def rs_copy(way, k, s):
        return remote(
            part.at[k, rs_rows(way, k, s)], rs.at[way, k, s - 1],
            rs_send.at[way, k, s - 1], rs_recv.at[way, k, s - 1], ring[way],
        )

    rsum, ho, io, stores = {}, [], [], []
    for k in range(CHUNKS):
        ag_step(k, NY // 2)
        hg[k].wait_recv()
        compute(k)
        for way in (UP, DOWN):
            rsum[way, k, 1] = start(rs_copy(way, k, 1))
        rows = pl.ds(pl.multiple_of(mine + k * size, size), size)
        ho.append(
            start(remote(hid.at[zo, pl.ds(k * size, size)], hid_out.at[rows], ho_send.at[k], ho_recv.at[k], partner))
        )
        stores.append(pltpu.make_async_copy(hid.at[zl, pl.ds(k * size, size)], hid_out.at[rows], store_sem.at[0, k]))
        stores[-1].start()

    for s in range(2, NY // 2 + 2):
        for k in range(CHUNKS):
            for way in (UP, DOWN):
                if s <= chain(way, k):
                    rsum[way, k, s - 1].wait_recv()
                    rows = rs_rows(way, k, s)
                    part[k, rows, :] = (
                        part[k, rows, :].astype(jnp.float32) + rs[way, k, s - 2].astype(jnp.float32)
                    ).astype(jnp.bfloat16)
                    rsum[way, k, s] = start(rs_copy(way, k, s))
            if s == NY // 2 + 1:
                total = part[k, pl.ds(pl.multiple_of(y * wide, wide), wide), :].astype(jnp.float32)
                for way in (UP, DOWN):
                    rsum[way, k, chain(way, k)].wait_recv()
                    total += rs[way, k, chain(way, k) - 1].astype(jnp.float32)
                fin[k] = total.astype(jnp.bfloat16)
                columns = pl.ds(pl.multiple_of(mine + k * size, size), size)
                own = fin.at[k, pl.ds(pl.multiple_of(zl * feats, feats), feats)]
                theirs = fin.at[k, pl.ds(pl.multiple_of(zo * feats, feats), feats)]
                io.append(start(remote(theirs, ig_out.at[:, columns], io_send.at[k], io_recv.at[k], partner)))
                stores.append(pltpu.make_async_copy(own, ig_out.at[:, columns], store_sem.at[1, k]))
                stores[-1].start()

    for copy in ho + io:
        copy.wait_recv()
    for copy in sent:
        copy.wait_send()
    for copy in stores:
        copy.wait()


def per_device(tokens, up_weight, hidden_grad):
    rows, feats = tokens.shape
    half = rows // 2
    size = half // CHUNKS
    wide = 2 * feats
    units = up_weight.shape[1]
    depth = NY * wide
    bf16, f32 = jnp.bfloat16, jnp.float32
    dma = pltpu.SemaphoreType.DMA
    hops = NY // 2
    flops = 2 * 2 * half * depth * 2 * units
    hidden, ig = pl.pallas_call(
        kernel,
        out_shape=(
            jax.ShapeDtypeStruct((rows, units), bf16),
            jax.ShapeDtypeStruct((feats, rows), bf16),
        ),
        in_specs=[pl.BlockSpec(memory_space=pl.ANY)] * 3,
        out_specs=[pl.BlockSpec(memory_space=pl.ANY)] * 2,
        scratch_shapes=[
            pltpu.VMEM((wide, half), bf16),
            pltpu.VMEM((NY, half, wide), bf16),
            pltpu.VMEM((2, NZH, NX, 2, up_weight.shape[0], units), bf16),
            pltpu.VMEM((2, half, units), bf16),
            pltpu.VMEM((2, half, units), bf16),
            pltpu.VMEM((2, size, units), f32),
            pltpu.VMEM((size, 2 * units), bf16),
            pltpu.VMEM((CHUNKS, depth, size), bf16),
            pltpu.VMEM((2, CHUNKS, hops, wide, size), bf16),
            pltpu.VMEM((CHUNKS, wide, size), bf16),
            dma((3,)),
            dma((CHUNKS,)), dma((CHUNKS,)),
            dma((NZ - 1,)), dma((NZ - 1,)),
            dma((NX - 1,)), dma((NX - 1,)),
            dma((NX,)), dma((NX,)),
            dma((CHUNKS,)), dma((CHUNKS,)),
            dma((2, CHUNKS, hops)), dma((2, CHUNKS, hops)),
            dma((2, CHUNKS, hops)), dma((2, CHUNKS, hops)),
            dma((CHUNKS,)), dma((CHUNKS,)),
            dma((CHUNKS,)), dma((CHUNKS,)),
            dma((2, CHUNKS)),
        ],
        compiler_params=pltpu.CompilerParams(
            collective_id=0, has_side_effects=True, vmem_limit_bytes=48 * 1024 * 1024
        ),
        cost_estimate=pl.CostEstimate(flops=flops, bytes_accessed=6 * rows * units, transcendentals=rows * units),
    )(jnp.transpose(tokens), up_weight, hidden_grad)
    return hidden, jnp.transpose(ig)


def solution(mesh):
    in_specs = (P("row", "col"), P("row", "col"), P("row", "col"))
    out_specs = (P("row", "col"), P("row", "col"))
    return jax.shard_map(
        per_device, mesh=mesh, in_specs=in_specs, out_specs=out_specs, check_vma=False
    )
```

time: 245 us -> 71 us (0.29)
  the two profiles are of different devices: /device:TPU:2 before, /device:TPU:16 now
where the time goes in v1:
time: 71 us; the launch traced here: 70.8 us
  Pallas kernels  65.6 us (92%)
  local copies, waits for them, and re-layouts  4.56 us (6%)
    pallas_call x1, Pallas kernels, per_device(): pl.pallas_call(kernel, out_shape=(jax.ShapeDtypeStruct((rows, units), bf1...  65.6 us
    unnamed x8, local copies, waits for them, and re-layouts  4.56 us

profile of v1, /device:TPU:16, one launch (start us, length us, event | category | flops | bytes accessed | tf_op | source)
XLA Modules:
  0.0 70.8 jit_solution(10040308989448932267)
XLA Ops:
  0.6 0.0 copy-start
  0.6 1.2 %copy-done = bf16[2048,256]{1,0:T(8,128)(2,1)S(1)} copy-done((bf16[2048,256]{1,0:T(8,128)(2,1)S(1)}, bf16[2048,256]{1,0:T(8,128)(2,1)}, u32[]{:S(2)}) %copy-start) | copy-done | bytes 1048600
  1.9 0.0 copy-start.1
  1.9 0.9 %copy-done.1 = bf16[2048,64]{0,1:T(8,128)(2,1)S(1)} copy-done((bf16[2048,64]{0,1:T(8,128)(2,1)S(1)}, bf16[2048,64]{0,1:T(8,128)(2,1)}, u32[]{:S(2)}) %copy-start.1) | copy-done | bytes 262168
  2.8 0.0 copy-start.2
  2.8 0.7 %copy-done.2 = bf16[32,256]{1,0:T(8,128)(2,1)S(1)} copy-done((bf16[32,256]{1,0:T(8,128)(2,1)S(1)}, bf16[32,256]{1,0:T(8,128)(2,1)}, u32[]{:S(2)}) %copy-start.2) | copy-done | bytes 16408
  3.5 65.6 %shard_map.50 = (bf16[2048,256]{1,0:T(8,128)(2,1)S(1)}, bf16[64,2048]{1,0:T(8,128)(2,1)S(1)}) custom-call(bf16[64,2048]{1,0:T(8,128)(2,1)S(1)} %bitcast.3, bf16[32,256]{1,0:T(8,128)(2,1)S(1)} %copy-done.2, bf16[2048,256]{1,0:T(8,128)(2,1)S(1)} %copy-done), custom_call_target="tpu_custom_call" | custom-call | flops 2147483648 | bytes 3145728 | tf_op jit(solution)/shard_map/pallas_call | solution.py:242
  69.1 1.0 %copy.7 = bf16[2048,256]{1,0:T(8,128)(2,1)} copy(bf16[2048,256]{1,0:T(8,128)(2,1)S(1)} %get-tuple-element.8) | data formatting | bytes 2097152
  70.1 0.7 copy.8
Async XLA Ops:
  0.6 1.2 %copy-start = (bf16[2048,256]{1,0:T(8,128)(2,1)S(1)}, bf16[2048,256]{1,0:T(8,128)(2,1)}, u32[]{:S(2)}) copy-start(bf16[2048,256]{1,0:T(8,128)(2,1)} %grad_in.1) | copy-start | bytes 3145732
  1.9 0.9 %copy-start.1 = (bf16[2048,64]{0,1:T(8,128)(2,1)S(1)}, bf16[2048,64]{0,1:T(8,128)(2,1)}, u32[]{:S(2)}) copy-start(bf16[2048,64]{0,1:T(8,128)(2,1)} %param.3) | copy-start | bytes 786436
  2.8 0.7 %copy-start.2 = (bf16[32,256]{1,0:T(8,128)(2,1)S(1)}, bf16[32,256]{1,0:T(8,128)(2,1)}, u32[]{:S(2)}) copy-start(bf16[32,256]{1,0:T(8,128)(2,1)} %w_in.1) | copy-start | bytes 49156

commit v2 on v0

v2 whole, which is shorter than its diff:
```python
import functools

import jax
import jax.numpy as jnp
from jax import lax
from jax.experimental import pallas as pl
from jax.experimental.pallas import tpu as pltpu
from jax.sharding import PartitionSpec as P

gelu_c = 0.7978845608028654
gelu_a = 0.044715

NZH, NX, NY = 4, 4, 8
NZ = 2 * NZH
CHUNKS, GROUP, EARLY = 8, 4, 4
HOPS = NY // 2
MESH = pl.DeviceIdType.MESH
UP, DOWN = 0, 1


def chain(way, k):
    return HOPS if (k % 2 == 0) == (way == UP) else HOPS - 1


def kernel(
    tok_in, w_in, grad_in, hid_out, ig_out,
    tok, wb, grad, hid, pre, pg, part, rs, fin,
    here, load_sem, tok_sem, tx_send, tx_recv, wz_send, wz_recv, wx_send, wx_recv, wc_send, wc_recv,
    hg_send, hg_recv, own_send, own_recv, ag_send, ag_recv, rs_send, rs_recv, ho_send, ho_recv, io_send, io_recv,
    store_sem,
):
    feats, half = tok_in.shape[0], tok_in.shape[1] // 2
    size = half // CHUNKS
    wide = 2 * feats
    depth, units = NY * wide, w_in.shape[1]
    r, c = lax.axis_index("row"), lax.axis_index("col")
    y, zl = lax.div(c, 2), lax.rem(c, 2)
    zh, x, core = lax.div(r, 2 * NX), lax.rem(lax.div(r, 2), NX), lax.rem(r, 2)
    zo = 1 - zl
    z = 2 * zh + zl
    mine, other = zl * half, zo * half
    own_rows = pl.ds(pl.multiple_of(zl * feats, feats), feats)
    their_rows = pl.ds(pl.multiple_of(zo * feats, feats), feats)

    def chunk(start, k, n=1):
        return pl.ds(pl.multiple_of(start + k * size, size), n * size)

    def at_y(step):
        return lax.rem(y + step + NY, NY)

    def z_device(step):
        there = lax.rem(z + step, NZ)
        return ((lax.div(there, 2) * NX + x) * 2 + core, 2 * y + lax.rem(there, 2))

    def x_device(step):
        return ((zh * NX + lax.rem(x + step, NX)) * 2 + core, c)

    ring = ((r, 2 * at_y(1) + zl), (r, 2 * at_y(-1) + zl))
    partner = (r, c + 1 - 2 * zl)
    sibling = (r + 1 - 2 * core, c)

    def remote(src, dst, send, recv, device):
        return pltpu.make_async_remote_copy(
            src_ref=src, dst_ref=dst, send_sem=send, recv_sem=recv, device_id=device, device_id_type=MESH
        )

    barrier = pltpu.get_barrier_semaphore()

    def signal(semaphore, device):
        pl.semaphore_signal(semaphore, inc=1, device_id=device, device_id_type=MESH)

    for device in (*ring, partner):
        signal(barrier, device)
    for d in range(1, NZ):
        pl.when(lax.div(lax.rem(z + d, NZ), 2) > zh)(functools.partial(signal, barrier, z_device(d)))
    for d in range(1, NX):
        pl.when(lax.rem(x + d, NX) < x)(functools.partial(signal, barrier, x_device(d)))
    pl.when(core == 1)(functools.partial(signal, barrier, sibling))

    def load_tokens(k):
        return pltpu.make_async_copy(tok_in.at[:, chunk(mine, k)], tok.at[k, y, own_rows], tok_sem.at[k])

    load_weights = pltpu.make_async_copy(w_in, wb.at[zl, zh, x, core], load_sem.at[0])
    load_grad = pltpu.make_async_copy(grad_in.at[chunk(mine, 0, CHUNKS)], grad.at[zl], load_sem.at[1])
    for k in range(CHUNKS):
        load_tokens(k).start()
    load_grad.start()

    load_weights.start()
    pl.semaphore_wait(barrier, 3 + 2 * zh + (NX - 1 - x) + (1 - core))
    for d in range(1, NZ):
        pl.when(lax.div(lax.rem(z + d, NZ), 2) < zh)(functools.partial(signal, here.at[0], z_device(d)))
    for d in range(1, NX):
        pl.when(lax.rem(x + d, NX) > x)(functools.partial(signal, here.at[1], x_device(d)))
    pl.when(core == 0)(functools.partial(signal, here.at[2], sibling))

    def wz_copy(d):
        return remote(w_in, wb.at[zl, zh, x, core], wz_send.at[d - 1], wz_recv.at[d - 1], z_device(d))

    def wx_copy(d):
        block = wb.at[:, :, x, core]
        return remote(block, block, wx_send.at[d - 1], wx_recv.at[d - 1], x_device(d))

    def wc_copy(d):
        block = wb.at[:, :, lax.rem(x + NX - d, NX), core]
        return remote(block, block, wc_send.at[d], wc_recv.at[d], sibling)

    def weights_z_known():
        for d in range(1, NZ):
            @pl.when(lax.div(lax.rem(z + d, NZ), 2) <= zh)
            def _():
                wz_copy(d).start()

    def weights_z():
        pl.when(zh < NZH - 1)(lambda: pl.semaphore_wait(here.at[0], NZ - 2 - 2 * zh))
        for d in range(1, NZ):
            @pl.when(lax.div(lax.rem(z + d, NZ), 2) > zh)
            def _():
                wz_copy(d).start()

    def weights_x():
        load_weights.wait()
        for d in range(1, NZ):
            wz_copy(d).wait_recv()
        pl.when(x > 0)(lambda: pl.semaphore_wait(here.at[1], x))
        for d in range(1, NX):
            wx_copy(d).start()
        pl.when(core == 1)(lambda: pl.semaphore_wait(here.at[2], 1))
        wc_copy(0).start()

    def weights_core():
        for d in range(1, NX):
            wx_copy(d).wait_recv()
            wc_copy(d).start()

    def weights_here():
        for d in range(NX):
            wc_copy(d).wait_recv()

    def weights_end():
        for d in range(1, NZ):
            wz_copy(d).wait_send()
        for d in range(1, NX):
            wx_copy(d).wait_send()
        for d in range(NX):
            wc_copy(d).wait_send()

    sent = []

    def start(copy):
        copy.start()
        sent.append(copy)
        return copy

    ag, own = {}, {}

    def ag_start(way, k, s):
        shard = tok.at[k, at_y(1 - s if way == UP else s - 1)]
        if s == 1 and k < EARLY:
            shard = shard.at[their_rows]
        ag[way, k, s] = start(
            remote(shard, shard, ag_send.at[way, k, s - 1], ag_recv.at[way, k, s - 1], ring[way])
        )

    def ag_step(k, s):
        for way in (UP, DOWN):
            if s <= chain(way, k):
                ag[way, k, s].wait_recv()
                if s == 1 and k < EARLY:
                    own[way, k].wait_recv()
            if s < chain(way, k):
                ag_start(way, k, s + 1)

    tx = []
    for k in range(CHUNKS):
        tx.append(
            start(
                remote(tok_in.at[:, chunk(other, k)], tok.at[k, y, own_rows], tx_send.at[k], tx_recv.at[k], partner)
            )
        )
        if k < EARLY:
            for way in (UP, DOWN):
                own[way, k] = start(
                    remote(
                        tok_in.at[:, chunk(mine, k)], tok.at[k, y, own_rows],
                        own_send.at[way, k], own_recv.at[way, k], ring[way],
                    )
                )

    weights_z_known()
    for k in range(CHUNKS):
        if k >= EARLY:
            load_tokens(k).wait()
        tx[k].wait_recv()
        for way in (UP, DOWN):
            ag_start(way, k, 1)

    hg = []
    for g in range(CHUNKS // GROUP):
        hg.append(
            start(
                remote(
                    grad_in.at[chunk(other, g * GROUP, GROUP)], grad.at[zl, chunk(0, g * GROUP, GROUP)],
                    hg_send.at[g], hg_recv.at[g], partner,
                )
            )
        )

    def compute(k):
        left = jnp.transpose(tok[k].reshape(depth, size))
        for b in range(2):
            pre[b] = jnp.dot(left, wb[b].reshape(depth, units), preferred_element_type=jnp.float32)

        @pl.loop(0, size // 32)
        def _(i):
            for b in range(2):
                rows = pl.ds(pl.multiple_of(i * 32, 32), 32)
                at = pl.ds(pl.multiple_of(k * size + i * 32, 32), 32)
                v = pre[b, rows, :]
                u = v * v
                t = jnp.tanh(v * (gelu_c + gelu_c * gelu_a * u))
                h = 0.5 + 0.5 * t
                slope = h + (0.5 * v) * (1.0 - t * t) * (gelu_c + 3.0 * gelu_c * gelu_a * u)
                hid[b, at, :] = (v * h).astype(jnp.bfloat16)
                pg[rows, b * units : (b + 1) * units] = (grad[b, at, :].astype(jnp.float32) * slope).astype(jnp.bfloat16)

        weights = jnp.concatenate([wb[b].reshape(depth, units) for b in range(2)], axis=1)
        part[k] = lax.dot_general(
            weights, pg[...], (((1,), (1,)), ((), ())), preferred_element_type=jnp.float32
        ).astype(jnp.bfloat16)

    ho, io, stores = [], [], []

    def store(src, dst, sem):
        stores.append(pltpu.make_async_copy(src, dst, sem))
        stores[-1].start()

    def hidden_out(k):
        rows = chunk(mine, k)
        ho.append(start(remote(hid.at[zo, chunk(0, k)], hid_out.at[rows], ho_send.at[k], ho_recv.at[k], partner)))
        store(hid.at[zl, chunk(0, k)], hid_out.at[rows], store_sem.at[0, k])

    rsum = {}

    def rs_rows(way, k, s):
        far_by = chain(way, k) - s + 1
        return pl.ds(pl.multiple_of(at_y(far_by if way == UP else -far_by) * wide, wide), wide)

    def rs_start(k, s):
        for way in (UP, DOWN):
            if s > chain(way, k):
                continue
            rows = rs_rows(way, k, s)
            if s > 1:
                rsum[way, k, s - 1].wait_recv()
                part[k, rows, :] = (
                    part[k, rows, :].astype(jnp.float32) + rs[way, k, s - 2].astype(jnp.float32)
                ).astype(jnp.bfloat16)
            rsum[way, k, s] = start(
                remote(
                    part.at[k, rows], rs.at[way, k, s - 1],
                    rs_send.at[way, k, s - 1], rs_recv.at[way, k, s - 1], ring[way],
                )
            )

    def finish(k):
        total = part[k, pl.ds(pl.multiple_of(y * wide, wide), wide), :].astype(jnp.float32)
        for way in (UP, DOWN):
            rsum[way, k, chain(way, k)].wait_recv()
            total += rs[way, k, chain(way, k) - 1].astype(jnp.float32)
        fin[k] = total.astype(jnp.bfloat16)
        columns = chunk(mine, k)
        io.append(start(remote(fin.at[k, their_rows], ig_out.at[:, columns], io_send.at[k], io_recv.at[k], partner)))
        store(fin.at[k, own_rows], ig_out.at[:, columns], store_sem.at[1, k])

    for k in (0, 1, 2, 3):
        ag_step(k, 1)
    for k in (4, 5):
        ag_step(k, 1)
    weights_z()
    for k in (0, 1, 2, 3):
        ag_step(k, 2)
    for k in (6, 7):
        ag_step(k, 1)
    weights_x()
    for k in (0, 1, 2, 3):
        ag_step(k, 3)
    for k in (4, 5, 6, 7):
        ag_step(k, 2)
    weights_core()
    for k in (4, 5, 6, 7):
        ag_step(k, 3)
    weights_here()
    load_grad.wait()
    hg[0].wait_recv()
    for k in (0, 1, 2, 3):
        ag_step(k, 4)
        if k < EARLY:
            load_tokens(k).wait()
        compute(k)
        rs_start(k, 1)
        hidden_out(k)
    hg[1].wait_recv()
    for k in (4, 5, 6, 7):
        rs_start(k - 4, 2)
        ag_step(k, 4)
        compute(k)
        rs_start(k, 1)
        hidden_out(k)
    for k in (0, 1, 2, 3):
        rs_start(k, 3)
    for k in (4, 5, 6, 7):
        rs_start(k, 2)
    for k in (4, 5, 6, 7):
        rs_start(k, 3)
    for k in range(CHUNKS):
        rs_start(k, 4)
    for k in range(CHUNKS):
        finish(k)

    for copy in ho + io:
        copy.wait_recv()
    for copy in sent:
        copy.wait_send()
    weights_end()
    for copy in stores:
        copy.wait()


def per_device(tokens, up_weight, hidden_grad):
    rows, feats = tokens.shape
    half = rows // 2
    size = half // CHUNKS
    wide = 2 * feats
    units = up_weight.shape[1]
    depth = NY * wide
    bf16, f32 = jnp.bfloat16, jnp.float32

    def pair(*shape):
        return [pltpu.SemaphoreType.DMA(shape)] * 2

    flops = 2 * 2 * half * depth * 2 * units
    hidden, ig = pl.pallas_call(
        kernel,
        out_shape=(
            jax.ShapeDtypeStruct((rows, units), bf16),
            jax.ShapeDtypeStruct((feats, rows), bf16),
        ),
        in_specs=[pl.BlockSpec(memory_space=pltpu.HBM)] * 3,
        out_specs=[pl.BlockSpec(memory_space=pl.ANY)] * 2,
        scratch_shapes=[
            pltpu.VMEM((CHUNKS, NY, wide, size), bf16),
            pltpu.VMEM((2, NZH, NX, 2, up_weight.shape[0], units), bf16),
            pltpu.VMEM((2, half, units), bf16),
            pltpu.VMEM((2, half, units), bf16),
            pltpu.VMEM((2, size, units), f32),
            pltpu.VMEM((size, 2 * units), bf16),
            pltpu.VMEM((CHUNKS, depth, size), bf16),
            pltpu.VMEM((2, CHUNKS, HOPS, wide, size), bf16),
            pltpu.VMEM((CHUNKS, wide, size), bf16),
            pltpu.SemaphoreType.REGULAR((3,)),
            pltpu.SemaphoreType.DMA((2,)),
            pltpu.SemaphoreType.DMA((CHUNKS,)),
            *pair(CHUNKS),
            *pair(NZ - 1),
            *pair(NX - 1),
            *pair(NX),
            *pair(CHUNKS // GROUP),
            *pair(2, EARLY),
            *pair(2, CHUNKS, HOPS),
            *pair(2, CHUNKS, HOPS),
            *pair(CHUNKS),
            *pair(CHUNKS),
            pltpu.SemaphoreType.DMA((2, CHUNKS)),
        ],
        compiler_params=pltpu.CompilerParams(
            collective_id=0, has_side_effects=True, vmem_limit_bytes=60 * 1024 * 1024
        ),
        cost_estimate=pl.CostEstimate(flops=flops, bytes_accessed=6 * rows * units, transcendentals=rows * units),
    )(jnp.transpose(tokens), up_weight, hidden_grad)
    return hidden, jnp.transpose(ig)


def solution(mesh):
    in_specs = (P("row", "col"), P("row", "col"), P("row", "col"))
    out_specs = (P("row", "col"), P("row", "col"))
    return jax.shard_map(
        per_device, mesh=mesh, in_specs=in_specs, out_specs=out_specs, check_vma=False
    )
```

time: 245 us -> 68.1 us (0.28)
  the two profiles are of different devices: /device:TPU:2 before, /device:TPU:392 now
where the time goes in v2:
time: 68.1 us; the launch traced here: 68 us
  Pallas kernels  64.3 us (94%)
  local copies, waits for them, and re-layouts  3.01 us (4%)
    pallas_call x1, Pallas kernels, per_device(): pl.pallas_call(kernel, out_shape=(jax.ShapeDtypeStruct((rows, units), bf1...  64.3 us
    unnamed x4, local copies, waits for them, and re-layouts  3.01 us

profile of v2, /device:TPU:392, one launch (start us, length us, event | category | flops | bytes accessed | tf_op | source)
XLA Modules:
  0.0 68.0 jit_solution(5203641343488687767)
XLA Ops:
  0.6 64.3 %shard_map.50 = (bf16[2048,256]{1,0:T(8,128)(2,1)}, bf16[64,2048]{1,0:T(8,128)(2,1)}) custom-call(bf16[64,2048]{1,0:T(8,128)(2,1)} %bitcast.3, bf16[32,256]{1,0:T(8,128)(2,1)} %w_in.1, bf16[2048,256]{1,0:T(8,128)(2,1)} %grad_in.1), custom_call_target="tpu_custom_call" | custom-call | flops 2147483648 | bytes 3145728 | tf_op jit(solution)/shard_map/pallas_call | solution.py:343
  64.9 0.0 copy-start
  64.9 2.3 %copy.7 = bf16[2048,256]{1,0:T(8,128)(2,1)} copy(bf16[2048,256]{1,0:T(8,128)(2,1)} %get-tuple-element.8) | data formatting | bytes 2097152
  67.3 0.0 copy-done
  67.3 0.7 %copy.8 = bf16[2048,64]{0,1:T(8,128)(2,1)} copy(bf16[2048,64]{0,1:T(8,128)(2,1)S(1)} %bitcast.2) | data formatting | bytes 524288
Async XLA Ops:
  64.9 2.3 %copy-start = (bf16[64,2048]{1,0:T(8,128)(2,1)S(1)}, bf16[64,2048]{1,0:T(8,128)(2,1)}, u32[]{:S(2)}) copy-start(bf16[64,2048]{1,0:T(8,128)(2,1)} %get-tuple-element.5) | copy-start | bytes 786436

commit v3 on v2

--- a/solution.py
+++ b/solution.py
@@ -13,6 +13,7 @@
 NZH, NX, NY = 4, 4, 8
 NZ = 2 * NZH
 CHUNKS, GROUP, EARLY = 8, 4, 4
+PIECES = 4
 HOPS = NY // 2
 MESH = pl.DeviceIdType.MESH
 UP, DOWN = 0, 1
@@ -207,11 +208,11 @@
         )
 
     def compute(k):
-        left = jnp.transpose(tok[k].reshape(depth, size))
+        left = jnp.concatenate([jnp.transpose(tok[k + i].reshape(depth, size)) for i in range(2)], axis=0)
         for b in range(2):
             pre[b] = jnp.dot(left, wb[b].reshape(depth, units), preferred_element_type=jnp.float32)
 
-        @pl.loop(0, size // 32)
+        @pl.loop(0, 2 * size // 32)
         def _(i):
             for b in range(2):
                 rows = pl.ds(pl.multiple_of(i * 32, 32), 32)
@@ -225,9 +226,11 @@
                 pg[rows, b * units : (b + 1) * units] = (grad[b, at, :].astype(jnp.float32) * slope).astype(jnp.bfloat16)
 
         weights = jnp.concatenate([wb[b].reshape(depth, units) for b in range(2)], axis=1)
-        part[k] = lax.dot_general(
+        terms = lax.dot_general(
             weights, pg[...], (((1,), (1,)), ((), ())), preferred_element_type=jnp.float32
         ).astype(jnp.bfloat16)
+        for i in range(2):
+            part[k + i] = terms[:, i * size : (i + 1) * size]
 
     ho, io, stores = [], [], []
 
@@ -290,23 +293,30 @@
     weights_core()
     for k in (4, 5, 6, 7):
         ag_step(k, 3)
+    for k in (0,):
+        ag_step(k, 4)
     weights_here()
     load_grad.wait()
     hg[0].wait_recv()
-    for k in (0, 1, 2, 3):
-        ag_step(k, 4)
-        if k < EARLY:
-            load_tokens(k).wait()
+    for k in (0, 2):
+        for i in (k, k + 1):
+            if i > 0:
+                ag_step(i, 4)
+            if i < EARLY:
+                load_tokens(i).wait()
         compute(k)
-        rs_start(k, 1)
-        hidden_out(k)
+        for i in (k, k + 1):
+            rs_start(i, 1)
+            hidden_out(i)
     hg[1].wait_recv()
-    for k in (4, 5, 6, 7):
-        rs_start(k - 4, 2)
-        ag_step(k, 4)
+    for k in (4, 6):
+        for i in (k, k + 1):
+            rs_start(i - 4, 2)
+            ag_step(i, 4)
         compute(k)
-        rs_start(k, 1)
-        hidden_out(k)
+        for i in (k, k + 1):
+            rs_start(i, 1)
+            hidden_out(i)
     for k in (0, 1, 2, 3):
         rs_start(k, 3)
     for k in (4, 5, 6, 7):
@@ -325,6 +335,24 @@
     weights_end()
     for copy in stores:
         copy.wait()
+
+
+def write(hid_in, ig_in, hid_out, ig_out, hid, ig, load_sem, store_sem):
+    rows, columns = hid_in.shape[0] // PIECES, ig_in.shape[1]
+    ways = []
+    for i in range(PIECES):
+        at = pl.ds(i * rows, rows)
+        ways.append((hid_in.at[at], hid.at[at], hid_out.at[at], i))
+    ways.append((ig_in, ig, ig_out, PIECES))
+    loads = [pltpu.make_async_copy(a, b, load_sem.at[i]) for a, b, _, i in ways]
+    stores = [pltpu.make_async_copy(b, c, store_sem.at[i]) for _, b, c, i in ways]
+    for load in loads:
+        load.start()
+    for load, store in zip(loads, stores):
+        load.wait()
+        store.start()
+    for store in stores:
+        store.wait()
 
 
 def per_device(tokens, up_weight, hidden_grad):
@@ -353,8 +381,8 @@
             pltpu.VMEM((2, NZH, NX, 2, up_weight.shape[0], units), bf16),
             pltpu.VMEM((2, half, units), bf16),
             pltpu.VMEM((2, half, units), bf16),
-            pltpu.VMEM((2, size, units), f32),
-            pltpu.VMEM((size, 2 * units), bf16),
+            pltpu.VMEM((2, 2 * size, units), f32),
+            pltpu.VMEM((2 * size, 2 * units), bf16),
             pltpu.VMEM((CHUNKS, depth, size), bf16),
             pltpu.VMEM((2, CHUNKS, HOPS, wide, size), bf16),
             pltpu.VMEM((CHUNKS, wide, size), bf16),
@@ -378,6 +406,16 @@
         ),
         cost_estimate=pl.CostEstimate(flops=flops, bytes_accessed=6 * rows * units, transcendentals=rows * units),
     )(jnp.transpose(tokens), up_weight, hidden_grad)
+    hidden, ig = pl.pallas_call(
+        write,
+        out_shape=(jax.ShapeDtypeStruct(hidden.shape, bf16), jax.ShapeDtypeStruct(ig.shape, bf16)),
+        in_specs=[pl.BlockSpec(memory_space=pl.ANY)] * 2,
+        out_specs=[pl.BlockSpec(memory_space=pl.ANY)] * 2,
+        scratch_shapes=[
+            pltpu.VMEM(hidden.shape, bf16), pltpu.VMEM(ig.shape, bf16),
+            *pair(PIECES + 1),
+        ],
+    )(hidden, ig)
     return hidden, jnp.transpose(ig)
 
 

time: 68.1 us -> 67.1 us (0.985)
  local copies, waits for them, and re-layouts: 3.01 us -> 0 us
  Pallas kernels: 64.3 us -> 66.3 us
    unnamed x4 -> x0, local copies, waits for them, and re-layouts: 3.01 us -> none
    pallas_call x0 -> x1, Pallas kernels: none -> 2.08 us  [per_device(): pl.pallas_call(write, out_shape=(jax.ShapeDtypeStruct(hidden.shape, bf16)...]
where the time goes in v3:
time: 67.1 us; the launch traced here: 66.9 us
  Pallas kernels  66.3 us (99%)
    pallas_call x1, Pallas kernels, per_device(): pl.pallas_call(kernel, out_shape=(jax.ShapeDtypeStruct((rows, units), bf1...  64.2 us
    pallas_call x1, Pallas kernels, per_device(): pl.pallas_call(write, out_shape=(jax.ShapeDtypeStruct(hidden.shape, bf16)...  2.08 us

profile of v3, /device:TPU:392, one launch (start us, length us, event | category | flops | bytes accessed | tf_op | source)
XLA Modules:
  0.0 66.9 jit_solution(5360692879143610210)
XLA Ops:
  0.6 64.2 %shard_map.50 = (bf16[2048,256]{1,0:T(8,128)(2,1)}, bf16[64,2048]{1,0:T(8,128)(2,1)}) custom-call(bf16[64,2048]{1,0:T(8,128)(2,1)} %bitcast.2, bf16[32,256]{1,0:T(8,128)(2,1)} %w_in.1, bf16[2048,256]{1,0:T(8,128)(2,1)} %grad_in.1), custom_call_target="tpu_custom_call" | custom-call | flops 2147483648 | bytes 3145728 | tf_op jit(solution)/shard_map/pallas_call | solution.py:371
  64.8 2.1 %shard_map.51 = (bf16[2048,256]{1,0:T(8,128)(2,1)}, bf16[64,2048]{1,0:T(8,128)(2,1)}) custom-call(bf16[2048,256]{1,0:T(8,128)(2,1)} %get-tuple-element.6.hid_in, bf16[64,2048]{1,0:T(8,128)(2,1)} %get-tuple-element.7.ig_in), custom_call_target="tpu_custom_call" | custom-call | tf_op jit(solution)/shard_map/pallas_call | solution.py:409
